TPU v7x, 512 devices: a whole 4x8x8 slice. The times are simulated.
512 devices in a mesh: section: 8 (over y), dp: 32 (over z_lo, x, core), tensor: 2 (over z_hi).
Axes of the slice: x: 4, y: 8, z: 8 (z_hi: 2, z_lo: 4; z = z_hi * 4 + z_lo), core: 2. Of those that a mesh axis runs over, the one named last changes fastest.
Arguments:
- context: bfloat16 [16384, 6144], P('dp', 'section'), may hold values from -64 to 64
- out_weight: bfloat16 [6144, 6144], P('section', ('tensor', 'dp')), may hold values from -0.078125 to 0.078125
- previous: bfloat16 [16384, 6144], P('dp', ('tensor', 'section')), may hold values from -64 to 64
- section_act: bfloat16 [8, 6144, 6144], P('section', 'dp', 'tensor'), may hold values from -6 to 6
- fresh_batch: bfloat16 [6144, 6144], P('dp', 'tensor'), may hold values from -6 to 6
- section_gains: float32 [8, 6144], P('section', 'tensor'), may hold values from 0.1 to 1.9
- mask_blocks: int32 [32, 12], P('dp'), may hold values from 0 to 15, all different within a row
Outputs:
- targets: bfloat16 [16384, 6144], P('dp', ('tensor', 'section'))
- section_out: bfloat16 [8, 6144, 6144], P('section', 'dp', 'tensor')
- target_error: float32 [6144, 6144], P('dp', ('tensor', 'section'))
Inputs may be any that keep to these rules, and one draw needn't show every extreme that they name: `mask_blocks`: each row names 12 different blocks.
All inputs are finite; a program needn't handle non-finite values.
Results may differ from a plain program's by a relative error of at most 0.015.
Values may be sent and summed in bfloat16 or wider, within the bound.
No kernel may reach another device: no remote copies, remote signals or barrier semaphores. Data moves between devices by JAX's collectives and lax.ppermute only.
A program may use at most 64 MiB of HBM per device.

v0:
```python
import jax
import jax.numpy as jnp
from jax import lax
from jax.sharding import PartitionSpec as P

GRID_SIDE = 16
BLOCK_SIDE = 4
PATCHES = 256


def shifted(value, axis, steps):
    count = lax.axis_size(axis)
    leading, last = (max(0, -steps), min(count, count - steps))
    return lax.ppermute(value, axis, [(source, source + steps) for source in range(leading, last)])


def spread_2(x, axis, root):
    mine = lax.axis_index(axis) == root
    return lax.psum(jnp.where(mine, x, jnp.zeros_like(x)), axis)


def instance_norm(values, images):
    shaped = values.reshape(images, -1, values.shape[-1])
    center = jnp.mean(shaped, axis=1, keepdims=True)
    spread = jnp.mean(jnp.square(shaped - center), axis=1, keepdims=True)
    return ((shaped - center) * lax.rsqrt(spread + 1e-05)).reshape(values.shape)


def masked_patches(mask_blocks):
    per_side = GRID_SIDE // BLOCK_SIDE
    within = jnp.arange(BLOCK_SIDE * BLOCK_SIDE, dtype=jnp.int32)
    chosen = mask_blocks[..., None]
    grid_row = chosen // per_side * BLOCK_SIDE + within // BLOCK_SIDE
    grid_col = chosen % per_side * BLOCK_SIDE + within % BLOCK_SIDE
    return grid_row * GRID_SIDE + grid_col


def on_device(context, out_weight, previous, section_act, fresh_batch, section_gains, mask_blocks):
    partial_sum = jnp.dot(
        context,
        lax.all_gather(out_weight, "dp", axis=1, tiled=True),
        preferred_element_type=jnp.float32,
    ).astype(jnp.bfloat16)
    width = previous.shape[1]
    position = lax.axis_index("section")
    sections = lax.axis_size("section")
    summed = lax.psum(partial_sum, "section").astype(jnp.float32)
    share = lax.dynamic_slice_in_dim(summed, position * width, width, 1)
    images = context.shape[0] // PATCHES
    normed_new = instance_norm(share, images)
    normed_old = instance_norm(previous.astype(jnp.float32), images)
    targets = (0.5 * (normed_new + normed_old)).astype(jnp.bfloat16)
    incoming = shifted(section_act, "section", 1)
    current = jnp.where(position == 0, fresh_batch[None], incoming).astype(jnp.float32)
    squares = lax.psum(jnp.sum(current * current, axis=-1), "tensor")
    features = current.shape[-1] * lax.axis_size("tensor")
    scaling = lax.rsqrt(squares[..., None] / features + 1e-06)
    section_out = (current * scaling * section_gains[:, None, :]).astype(jnp.bfloat16)
    predicted = spread_2(section_act[0], "section", sections - 1)
    own_columns = lax.dynamic_slice_in_dim(predicted, position * width, width, 1)
    patch_ids = masked_patches(mask_blocks[0]).reshape(-1)
    picked = jnp.take(targets, patch_ids, axis=0).astype(jnp.float32)
    target_error = own_columns.astype(jnp.float32) - picked
    return (targets, section_out, target_error)


def solution(mesh):
    in_specs = (
        P("dp", "section"),
        P("section", ("tensor", "dp")),
        P("dp", ("tensor", "section")),
        P("section", "dp", "tensor"),
        P("dp", "tensor"),
        P("section", "tensor"),
        P("dp", None),
    )
    out_specs = (
        P("dp", ("tensor", "section")),
        P("section", "dp", "tensor"),
        P("dp", ("tensor", "section")),
    )
    return jax.shard_map(
        on_device, mesh=mesh, in_specs=in_specs, out_specs=out_specs, check_vma=False
    )
```

profile of v0, /device:TPU:1, one launch (start us, length us, event | category | flops | bytes accessed | tf_op | source)
XLA Modules:
  0.0 233.4 jit_solution(17504914805390724261)
XLA Ops:
  7.2 0.0 copy-start
  7.2 0.0 all-gather.2.cloned.1.call-start
  7.2 0.7 all-gather.2.cloned.1.call-update
  7.9 0.0 all-reduce.3.cloned.1.call-start
  8.0 1.2 select_bitcast_fusion
  9.2 73.9 %all-gather.2.cloned.1.call-done = bf16[768,3072]{0,1:T(8,128)(2,1)} async-done(((bf16[768,96]{0,1:T(8,128)(2,1)}), bf16[768,3072]{0,1:T(8,128)(2,1)}) %all-gather.2.cloned.1.call-update) | async-done | bytes 4718608 | tf_op jit(solution)/shard_map/all_gather | solution.py:41
  83.1 0.0 copy-done
  83.1 6.3 %convolution_convert_fusion = bf16[512,3072]{1,0:T(8,128)(2,1)} fusion(bf16[512,768]{1,0:T(8,128)(2,1)S(1)} %copy-done, bf16[768,3072]{0,1:T(8,128)(2,1)} %all-gather.2.cloned.1.call-done), kind=kOutput, calls=%fused_computation.1 | convolution fusion | flops 2417491968 | bytes 8650752 | tf_op jit(solution)/shard_map/dot_general | solution.py:39
  89.4 0.0 all-reduce.3.cloned.1.call-update
  89.4 3.3 %collective-permute-start = (bf16[1,192,3072]{2,1,0:T(8,128)(2,1)}, bf16[1,192,3072]{2,1,0:T(8,128)(2,1)S(1)}, u32[]{:S(2)}, u32[]{:S(2)}) collective-permute-start(bf16[1,192,3072]{2,1,0:T(8,128)(2,1)} %param.10), channel_id=1, source_target_pairs={{0,64},{64,128},{128,192},{192,256},{256,320},{320,384},{384,448},... | collective-permute-start | bytes 3538952 | tf_op jit(solution)/shard_map/ppermute | solution.py:14
  92.8 0.0 copy-done.6
  92.8 0.1 add_add_fusion
  92.9 0.1 add.181
  92.9 0.6 add.178
  93.6 0.6 pad_clamp_fusion
  94.2 0.1 bitcast_reduce_fusion
  94.3 0.1 fusion.7
  94.4 1.2 compare_and_fusion
  95.6 0.6 add_rsqrt_fusion
  96.2 38.2 %collective-permute-done = bf16[1,192,3072]{2,1,0:T(8,128)(2,1)S(1)} collective-permute-done((bf16[1,192,3072]{2,1,0:T(8,128)(2,1)}, bf16[1,192,3072]{2,1,0:T(8,128)(2,1)S(1)}, u32[]{:S(2)}, u32[]{:S(2)}) %collective-permute-start) | collective-permute-done | bytes 1179680 | tf_op jit(solution)/shard_map/ppermute | solution.py:14
  134.4 1.0 fusion
  135.5 8.4 %psum.22 = f32[1,192]{1,0:T(1,128)} all-reduce(f32[1,192]{1,0:T(1,128)} %bitcast.67), channel_id=1, replica_groups=mesh['section'=8,'dp'=32,'tensor'=2] {'tensor'}, use_global_device_ids=true, to_apply=%region_6.7 | all-reduce | flops 192 | bytes 1536 | tf_op jit(solution)/shard_map/psum | solution.py:55
  143.8 0.7 add_rsqrt_fusion.2
  144.5 0.0 copy-done.4
  144.5 1.5 fusion.2
  146.0 74.2 %all-reduce.3.cloned.1.call-done = (bf16[512,3072]{1,0:T(8,128)(2,1)}, bf16[192,3072]{1,0:T(8,128)(2,1)}) async-done(((bf16[512,3072]{1,0:T(8,128)(2,1)}, bf16[192,3072]{1,0:T(8,128)(2,1)}), (bf16[512,3072]{1,0:T(8,128)(2,1)}, bf16[192,3072]{1,0:T(8,128)(2,1)})) %all-reduce.3.cloned.1.call-update) | async-done | bytes 4325392 | tf_op jit(solution)/shard_map/psum | solution.py:47
  220.2 1.1 bitcast_reduce_fusion.1
  221.3 1.1 fusion.9
  222.4 1.2 fusion.5
  223.7 0.0 copy-start.1
  223.7 1.2 gather_fusion
  224.8 1.7 convert_subtract_fusion
  (15 shorter events, 0.1 us)
Async XLA Ops:
  7.2 75.9 %copy-start = (bf16[512,768]{1,0:T(8,128)(2,1)S(1)}, bf16[512,768]{1,0:T(8,128)(2,1)}, u32[]{:S(2)}) copy-start(bf16[512,768]{1,0:T(8,128)(2,1)} %param.7) | copy-start | bytes 2359300
  7.2 75.9 %all-gather.2.cloned.1.call-start = ((), (), s32[]{:S(2)}) async-start(), calls=%async_computation | async-start | bytes 4866048 | tf_op jit(solution)/shard_map/all_gather | solution.py:41
  7.9 212.3 %all-reduce.3.cloned.1.call-start = ((), (), s32[]{:S(2)}) async-start(), calls=%async_computation.1 | async-start | bytes 8650752 | tf_op jit(solution)/shard_map/psum | solution.py:47
  89.4 3.4 %copy-start.6 = (s32[1,12]{1,0:T(1,128)S(1)}, s32[1,12]{1,0:T(1,128)}, u32[]{:S(2)}) copy-start(s32[1,12]{1,0:T(1,128)} %param.13) | copy-start | bytes 148
  89.4 4.8 %copy-start.3 = (bf16[512,384]{1,0:T(8,128)(2,1)S(1)}, bf16[512,384]{1,0:T(8,128)(2,1)}, u32[]{:S(2)}) copy-start(bf16[512,384]{1,0:T(8,128)(2,1)} %param.9) | copy-start | bytes 1179652
  89.4 45.0 %copy-start.2 = (bf16[192,3072]{1,0:T(8,128)(2,1)S(1)}, bf16[192,3072]{1,0:T(8,128)(2,1)}, u32[]{:S(2)}) copy-start(bf16[192,3072]{1,0:T(8,128)(2,1)} %param.11) | copy-start | bytes 3538948
  89.4 45.0 %collective-permute-start = (bf16[1,192,3072]{2,1,0:T(8,128)(2,1)}, bf16[1,192,3072]{2,1,0:T(8,128)(2,1)S(1)}, u32[]{:S(2)}, u32[]{:S(2)}) collective-permute-start(bf16[1,192,3072]{2,1,0:T(8,128)(2,1)} %param.10), channel_id=1, source_target_pairs={{0,64},{64,128},{128,192},{192,256},{256,320},{320,384},{384,448},... | collective-permute-start | bytes 3538952 | tf_op jit(solution)/shard_map/ppermute | solution.py:14
  93.6 50.9 %copy-start.4 = (f32[1,3072]{1,0:T(1,128)S(1)}, f32[1,3072]{1,0:T(1,128)}, u32[]{:S(2)}) copy-start(f32[1,3072]{1,0:T(1,128)} %param.12) | copy-start | bytes 36868
  146.0 78.8 %copy-start.5 = (pred[192]{0:T(512)(128)(4,1)S(1)}, pred[192]{0:T(512)(128)(4,1)}, u32[]{:S(2)}) copy-start(pred[192]{0:T(512)(128)(4,1)} %compare_and_fusion) | copy-start | bytes 580
  223.7 2.9 %copy-start.1 = (bf16[512,384]{1,0:T(8,128)(2,1)}, bf16[512,384]{1,0:T(8,128)(2,1)S(1)}, u32[]{:S(2)}) copy-start(bf16[512,384]{1,0:T(8,128)(2,1)S(1)} %fusion.5) | copy-start | bytes 1179652
Sparse Core Ops, SparseCore 0:
  10.2 72.8 all-gather.1
  89.5 130.6 all-reduce.2
where the time goes:
time: 234 us; the launch traced here: 233 us
  waiting for transfers between devices  187 us (80%)
  between operations  14.1 us (6%)
  other arithmetic  12.4 us (5%)
  blocking collectives  8.36 us (4%)
  matrix products  6.33 us (3%)
  starting transfers between devices  3.39 us (1%)
    psum x1, waiting for transfers between devices, on_device(): summed = lax.psum(partial_sum, 'section').astype(jnp.float32)  74.2 us
    all_gather x1, waiting for transfers between devices, on_device(): lax.all_gather(out_weight, 'dp', axis=1, tiled=True)  73.9 us
    ppermute x1, waiting for transfers between devices, shifted(): lax.ppermute(value, axis, [(source, source + steps) for source in range(l...  38.2 us
    psum x1, blocking collectives, on_device(): squares = lax.psum(jnp.sum(current * current, axis=-1), 'tensor')  8.36 us
    dot_general x1, matrix products, on_device(): jnp.dot(context, lax.all_gather(out_weight, 'dp', axis=1, tiled=True), pr...  6.33 us
  transfers between devices with their start and end apart: 3, of which 3 were waited for; matrix products, arithmetic and copies ran while one was open for 3% of the time, Pallas kernels for 0%

commit v1 on v0

--- a/solution.py
+++ b/solution.py
@@ -38,7 +38,9 @@
 def on_device(context, out_weight, previous, section_act, fresh_batch, section_gains, mask_blocks):
     partial_sum = jnp.dot(
         context,
-        lax.all_gather(out_weight, "dp", axis=1, tiled=True),
+        jnp.concatenate(
+            lax.all_to_all(jnp.stack([out_weight] * lax.axis_size("dp")), "dp", 0, 0), axis=1
+        ),
         preferred_element_type=jnp.float32,
     ).astype(jnp.bfloat16)
     width = previous.shape[1]

time: 234 us -> 281 us (1.20)
  waiting for transfers between devices: 187 us -> 218 us
  starting transfers between devices: 3.39 us -> 15 us
  local copies, waits for them, and re-layouts: 1.91 us -> 5.6 us
    all_to_all x0 -> x1, waiting for transfers between devices: none -> 104 us  [on_device(): lax.all_to_all(jnp.stack([out_weight] * lax.axis_size('dp')), 'dp', 0, 0)]
    all_gather x1 -> x0, waiting for transfers between devices: 73.9 us -> none  [on_device(): lax.all_gather(out_weight, 'dp', axis=1, tiled=True)]
    all_to_all x0 -> x1, starting transfers between devices: none -> 11.6 us  [on_device(): lax.all_to_all(jnp.stack([out_weight] * lax.axis_size('dp')), 'dp', 0, 0)]
    psum x1, waiting for transfers between devices: 74.2 us -> 80.6 us  [on_device(): summed = lax.psum(partial_sum, 'section').astype(jnp.float32)]
    ppermute x1, waiting for transfers between devices: 38.2 us -> 33.3 us  [shifted(): lax.ppermute(value, axis, [(source, source + steps) for source in range(l...]
    another operation x0 -> x1, local copies, waits for them, and re-layouts: none -> 3.69 us  [on_device(): jnp.stack([out_weight] * lax.axis_size('dp'))]
where the time goes in v1:
time: 281 us
  waiting for transfers between devices  218 us (78%)
  starting transfers between devices  15 us (5%)
  between operations  14.1 us (5%)
  other arithmetic  12.2 us (4%)
  blocking collectives  9.74 us (3%)
  matrix products  6.33 us (2%)
  local copies, waits for them, and re-layouts  5.6 us (2%)
    all_to_all x1, waiting for transfers between devices, on_device(): lax.all_to_all(jnp.stack([out_weight] * lax.axis_size('dp')), 'dp', 0, 0)  104 us
    psum x1, waiting for transfers between devices, on_device(): summed = lax.psum(partial_sum, 'section').astype(jnp.float32)  80.6 us
    ppermute x1, waiting for transfers between devices, shifted(): lax.ppermute(value, axis, [(source, source + steps) for source in range(l...  33.3 us
    all_to_all x1, starting transfers between devices, on_device(): lax.all_to_all(jnp.stack([out_weight] * lax.axis_size('dp')), 'dp', 0, 0)  11.6 us
    psum x1, blocking collectives, on_device(): squares = lax.psum(jnp.sum(current * current, axis=-1), 'tensor')  9.74 us
    dot_general x1, matrix products, on_device(): jnp.dot(context, jnp.concatenate(lax.all_to_all(jnp.stack([out_weight] *...  6.33 us
  transfers between devices with their start and end apart: 3, of which 3 were waited for; matrix products, arithmetic and copies ran while one was open for 3% of the time, Pallas kernels for 0%

profile of v1, /device:TPU:1, one launch (start us, length us, event | category | flops | bytes accessed | tf_op | source)
XLA Modules:
  0.0 280.6 jit_solution(11682268863090875007)
XLA Ops:
  7.2 0.0 copy-start
  7.2 3.7 %stack.2 = bf16[32,768,96]{1,2,0:T(8,128)(2,1)} broadcast(bf16[768,96]{0,1:T(8,128)(2,1)} %param.8), dimensions={1,2} | broadcast | bytes 4866048 | tf_op jit(solution)/shard_map/stack | solution.py:42
  10.9 11.6 %all-to-all-start = ((bf16[32,768,96]{1,2,0:T(8,128)(2,1)}), bf16[32,768,96]{1,2,0:T(8,128)(2,1)}, u32[]{:S(2)}, u32[]{:S(2)}) async-start(bf16[32,768,96]{1,2,0:T(8,128)(2,1)} %stack.2), calls=%async_computation | async-start | bytes 9437184 | tf_op jit(solution)/shard_map/all_to_all | solution.py:42
  22.4 0.0 all-reduce.3.cloned.1.call-start
  22.5 0.0 copy-done.4
  22.5 1.1 select_bitcast_fusion
  23.6 103.6 %all-to-all-done = bf16[32,768,96]{1,2,0:T(8,128)(2,1)} async-done(((bf16[32,768,96]{1,2,0:T(8,128)(2,1)}), bf16[32,768,96]{1,2,0:T(8,128)(2,1)}, u32[]{:S(2)}, u32[]{:S(2)}) %all-to-all-start) | async-done | bytes 4718624 | tf_op jit(solution)/shard_map/all_to_all | solution.py:42
  127.2 0.0 copy-done
  127.2 6.3 %convolution_convert_fusion = bf16[512,3072]{1,0:T(8,128)(2,1)} fusion(bf16[512,768]{1,0:T(8,128)(2,1)S(1)} %copy-done, bf16[768,3072]{0,1:T(8,128)(2,1)} %bitcast.1), kind=kOutput, calls=%fused_computation.1 | convolution fusion | flops 2417491968 | bytes 8650752 | tf_op jit(solution)/shard_map/dot_general | solution.py:39
  133.5 0.0 all-reduce.3.cloned.1.call-update
  133.6 3.4 %collective-permute-start = (bf16[1,192,3072]{2,1,0:T(8,128)(2,1)}, bf16[1,192,3072]{2,1,0:T(8,128)(2,1)S(1)}, u32[]{:S(2)}, u32[]{:S(2)}) collective-permute-start(bf16[1,192,3072]{2,1,0:T(8,128)(2,1)} %param.10), channel_id=1, source_target_pairs={{0,64},{64,128},{128,192},{192,256},{256,320},{320,384},{384,448},... | collective-permute-start | bytes 3538952 | tf_op jit(solution)/shard_map/ppermute | solution.py:14
  137.0 0.1 add_add_fusion
  137.1 0.1 add.181
  137.2 0.6 add.178
  137.8 0.6 pad_clamp_fusion
  138.4 0.1 bitcast_reduce_fusion
  138.5 0.1 fusion.7
  138.7 1.2 compare_and_fusion
  139.9 0.6 add_rsqrt_fusion
  140.5 33.3 %collective-permute-done = bf16[1,192,3072]{2,1,0:T(8,128)(2,1)S(1)} collective-permute-done((bf16[1,192,3072]{2,1,0:T(8,128)(2,1)}, bf16[1,192,3072]{2,1,0:T(8,128)(2,1)S(1)}, u32[]{:S(2)}, u32[]{:S(2)}) %collective-permute-start) | collective-permute-done | bytes 1179680 | tf_op jit(solution)/shard_map/ppermute | solution.py:14
  173.8 1.0 fusion
  174.8 9.7 %psum.22 = f32[1,192]{1,0:T(1,128)} all-reduce(f32[1,192]{1,0:T(1,128)} %bitcast.70), channel_id=1, replica_groups=mesh['section'=8,'dp'=32,'tensor'=2] {'tensor'}, use_global_device_ids=true, to_apply=%region_6.7 | all-reduce | flops 192 | bytes 1536 | tf_op jit(solution)/shard_map/psum | solution.py:57
  184.5 0.7 add_rsqrt_fusion.2
  185.2 1.5 fusion.2
  186.7 80.6 %all-reduce.3.cloned.1.call-done = (bf16[512,3072]{1,0:T(8,128)(2,1)}, bf16[192,3072]{1,0:T(8,128)(2,1)}) async-done(((bf16[512,3072]{1,0:T(8,128)(2,1)}, bf16[192,3072]{1,0:T(8,128)(2,1)}), (bf16[512,3072]{1,0:T(8,128)(2,1)}, bf16[192,3072]{1,0:T(8,128)(2,1)})) %all-reduce.3.cloned.1.call-update) | async-done | bytes 4325392 | tf_op jit(solution)/shard_map/psum | solution.py:49
  267.3 1.1 bitcast_reduce_fusion.1
  268.4 1.1 fusion.9
  269.6 1.2 fusion.5
  270.8 0.0 copy-start.1
  270.8 1.2 gather_fusion
  272.0 1.7 convert_subtract_fusion
  273.7 0.0 copy-done.1
  (17 shorter events, 0.1 us)
Async XLA Ops:
  7.2 120.0 %copy-start = (bf16[512,768]{1,0:T(8,128)(2,1)S(1)}, bf16[512,768]{1,0:T(8,128)(2,1)}, u32[]{:S(2)}) copy-start(bf16[512,768]{1,0:T(8,128)(2,1)} %param.7) | copy-start | bytes 2359300
  10.9 11.6 %copy-start.4 = (bf16[1,192,3072]{2,1,0:T(8,128)(2,1)S(1)}, bf16[1,192,3072]{2,1,0:T(8,128)(2,1)}, u32[]{:S(2)}) copy-start(bf16[1,192,3072]{2,1,0:T(8,128)(2,1)} %param.10) | copy-start | bytes 3538948
  10.9 116.3 %all-to-all-start = ((bf16[32,768,96]{1,2,0:T(8,128)(2,1)}), bf16[32,768,96]{1,2,0:T(8,128)(2,1)}, u32[]{:S(2)}, u32[]{:S(2)}) async-start(bf16[32,768,96]{1,2,0:T(8,128)(2,1)} %stack.2), calls=%async_computation | async-start | bytes 9437184 | tf_op jit(solution)/shard_map/all_to_all | solution.py:42
  22.4 244.9 %all-reduce.3.cloned.1.call-start = ((), (), s32[]{:S(2)}) async-start(), calls=%async_computation.1 | async-start | bytes 8650752 | tf_op jit(solution)/shard_map/psum | solution.py:49
  133.5 3.5 %copy-start.7 = (s32[1,12]{1,0:T(1,128)S(1)}, s32[1,12]{1,0:T(1,128)}, u32[]{:S(2)}) copy-start(s32[1,12]{1,0:T(1,128)} %param.13) | copy-start | bytes 148
  133.5 4.9 %copy-start.3 = (bf16[512,384]{1,0:T(8,128)(2,1)S(1)}, bf16[512,384]{1,0:T(8,128)(2,1)}, u32[]{:S(2)}) copy-start(bf16[512,384]{1,0:T(8,128)(2,1)} %param.9) | copy-start | bytes 1179652
  133.5 40.2 %copy-start.2 = (bf16[192,3072]{1,0:T(8,128)(2,1)S(1)}, bf16[192,3072]{1,0:T(8,128)(2,1)}, u32[]{:S(2)}) copy-start(bf16[192,3072]{1,0:T(8,128)(2,1)} %param.11) | copy-start | bytes 3538948
  133.6 40.2 %collective-permute-start = (bf16[1,192,3072]{2,1,0:T(8,128)(2,1)}, bf16[1,192,3072]{2,1,0:T(8,128)(2,1)S(1)}, u32[]{:S(2)}, u32[]{:S(2)}) collective-permute-start(bf16[1,192,3072]{2,1,0:T(8,128)(2,1)} %param.10), channel_id=1, source_target_pairs={{0,64},{64,128},{128,192},{192,256},{256,320},{320,384},{384,448},... | collective-permute-start | bytes 3538952 | tf_op jit(solution)/shard_map/ppermute | solution.py:14
  137.8 47.4 %copy-start.5 = (f32[1,3072]{1,0:T(1,128)S(1)}, f32[1,3072]{1,0:T(1,128)}, u32[]{:S(2)}) copy-start(f32[1,3072]{1,0:T(1,128)} %param.12) | copy-start | bytes 36868
  186.7 85.2 %copy-start.6 = (pred[192]{0:T(512)(128)(4,1)S(1)}, pred[192]{0:T(512)(128)(4,1)}, u32[]{:S(2)}) copy-start(pred[192]{0:T(512)(128)(4,1)} %compare_and_fusion) | copy-start | bytes 580
  270.8 2.9 %copy-start.1 = (bf16[512,384]{1,0:T(8,128)(2,1)}, bf16[512,384]{1,0:T(8,128)(2,1)S(1)}, u32[]{:S(2)}) copy-start(bf16[512,384]{1,0:T(8,128)(2,1)S(1)} %fusion.5) | copy-start | bytes 1179652
Sparse Core Ops, SparseCore 0:
  133.7 133.6 all-reduce.2
